TPU v7x, 32 devices: a whole 2x2x4 slice. The times are simulated.
32 devices in a mesh: dp: 16 (over z, y, x), proto: 2 (over core).
Axes of the slice: x: 2, y: 2, z: 4, core: 2. Of those that a mesh axis runs over, the one named last changes fastest.
Arguments:
- teacher: bfloat16 [4096, 128], P('dp'), may hold values from -1000 to 1000
- student: bfloat16 [4096, 128], P('dp'), may hold values from -1000 to 1000
- prototypes: bfloat16 [128, 65536], P('dp', 'proto'), may hold values from -1 to 1, as said below
Outputs:
- crop_loss: float32 [4096], P('dp')
- logit_grad: bfloat16 [4096, 65536], P('dp', 'proto')
- proto_grad: bfloat16 [128, 65536], P('dp', 'proto')
Inputs may be any that keep to these rules, and one draw needn't show every extreme that they name: `prototypes`: prototype columns have unit length.
All inputs are finite; a program needn't handle non-finite values.
Results may differ from a plain program's by a relative error of at most 0.015.
Values may be sent and summed in bfloat16 or wider, within the bound.
No kernel may reach another device: no remote copies, remote signals or barrier semaphores. Data moves between devices by JAX's collectives and lax.ppermute only.
A program may use at most 128 MiB of HBM per device.

v0:
```python
import jax
import jax.numpy as jnp
from jax import lax
from jax.sharding import PartitionSpec as P

ITERS = 3


def rounded_term(stud_cols, logit_grad):
    term = lax.dot_general(
        stud_cols, logit_grad, (((0,), (0,)), ((), ())), preferred_element_type=jnp.float32
    )
    return lax.optimization_barrier(term.astype(jnp.bfloat16)).astype(jnp.float32)


def shards(teacher, student, prototypes):
    width_local = prototypes.shape[1]
    rows_here = teacher.shape[0]
    crops_all = rows_here * lax.axis_size("dp")
    protos_all = width_local * lax.axis_size("proto")
    shard_rows = lax.all_gather(prototypes, "dp", axis=0, tiled=True)
    stud_cols = student
    teach_scores = jnp.dot(teacher, shard_rows, preferred_element_type=jnp.float32)
    stud_scores = jnp.dot(stud_cols, shard_rows, preferred_element_type=jnp.float32)
    teach_peak, stud_peak = lax.pmax(
        (jnp.max(teach_scores, axis=1), jnp.max(stud_scores, axis=1)), "proto"
    )
    teach_exp = jnp.exp(teach_scores - teach_peak[:, None])
    stud_exp = jnp.exp(stud_scores - stud_peak[:, None])
    row_scale = 1.0 / lax.psum(jnp.sum(teach_exp, axis=1), "proto")

    def column_scale(scale_in):
        partial_value = jnp.sum(teach_exp * scale_in[:, None], axis=0)
        return 1.0 / (protos_all * lax.psum(partial_value, "dp"))

    def row_total(weighted_in):
        return lax.psum(jnp.sum(weighted_in, axis=1), "proto")

    for sweep_index in range(ITERS - 1):
        col_scale = column_scale(row_scale)
        row_scale = 1.0 / (crops_all * row_total(teach_exp * col_scale[None, :]))
    col_scale = column_scale(row_scale)
    weighted = teach_exp * col_scale[None, :]
    row_scale = 1.0 / (crops_all * row_total(weighted))
    targets = weighted * (crops_all * row_scale)[:, None]
    stud_total = lax.psum(jnp.sum(stud_exp, axis=1), "proto")
    log_probs = stud_scores - stud_peak[:, None] - jnp.log(stud_total)[:, None]
    crop_loss = -lax.psum(jnp.sum(targets * log_probs, axis=1), "proto")
    softmax_rows = stud_exp / stud_total[:, None]
    logit_grad = (protos_all * (softmax_rows - targets)).astype(jnp.bfloat16)
    stud_cols = student
    summed = lax.psum_scatter(
        rounded_term(stud_cols, logit_grad), "dp", scatter_dimension=0, tiled=True
    )
    return (crop_loss, logit_grad, (summed / 128.0).astype(jnp.bfloat16))


def solution(mesh):
    placed = (P("dp", None), P("dp", None), P("dp", "proto"))
    return jax.shard_map(
        shards,
        mesh=mesh,
        in_specs=placed,
        out_specs=(P("dp"), P("dp", "proto"), P("dp", "proto")),
        check_vma=False,
    )
```

profile of v0, /device:TPU:0, one launch (start us, length us, event | category | flops | bytes accessed | tf_op | source)
XLA Modules:
  0.0 1016.9 jit_solution(10112712267481014478)
XLA Ops:
  8.0 118.4 %all-gather.2.cloned.1.call-done = bf16[128,32768]{1,0:T(8,128)(2,1)} async-done(((bf16[8,32768]{1,0:T(8,128)(2,1)}), bf16[128,32768]{1,0:T(8,128)(2,1)}) %all-gather.2.cloned.1.call-update) | async-done | bytes 8388624 | tf_op jit(solution)/shard_map/all_gather | solution.py:21
  126.3 19.2 %fusion.3 = (f32[256]{0:T(256)S(1)}, f32[256,32768]{1,0:T(8,128)}) fusion(bf16[256,128]{1,0:T(8,128)(2,1)} %param.3, bf16[128,32768]{1,0:T(8,128)(2,1)} %all-gather.2.cloned.1.call-done), kind=kOutput, calls=%fused_computation.22 | convolution fusion | flops 2155872000 | bytes 42009600 | tf_op jit(solution)/shard_map/dot_general | solution.py:23
  145.5 13.1 %fusion.2 = (f32[256]{0:T(256)S(1)}, f32[256,32768]{1,0:T(8,128)}) fusion(bf16[256,128]{1,0:T(8,128)(2,1)S(1)} %copy-done, bf16[128,32768]{1,0:T(8,128)(2,1)S(1)} %copy-done.1), kind=kOutput, calls=%fused_computation.21 | convolution fusion | flops 2155872000 | bytes 42009600 | tf_op jit(solution)/shard_map/dot_general | solution.py:24
  161.0 13.6 %fusion.1 = f32[256]{0:T(256)S(1)} fusion(f32[256,32768]{1,0:T(8,128)} %get-tuple-element.18, f32[256]{0:T(256)S(1)} %get-tuple-element.12), kind=kLoop, calls=%fused_computation.20 | loop fusion | flops 16776960 | bytes 33556480 | tf_op jit(solution)/shard_map/reduce_sum | solution.py:30
  177.1 15.2 %multiply_reduce_fusion.5 = f32[32768]{0:T(1024)} fusion(f32[256]{0:T(256)S(1)} %broadcast_divide_fusion, f32[256,32768]{1,0:T(8,128)} %get-tuple-element.18, f32[256]{0:T(256)S(1)} %get-tuple-element.12), kind=kLoop, calls=%fused_computation.8 | loop fusion | flops 25133056 | bytes 33687552 | tf_op jit(solution)/shard_map/reduce_sum | solution.py:33
  192.4 102.5 %all-reduce.6.cloned.1.call-done = f32[32768]{0:T(1024)} async-done(((f32[32768]{0:T(1024)}), f32[32768]{0:T(1024)}) %all-reduce.6.cloned.1.call-update) | async-done | bytes 131088 | tf_op jit(solution)/shard_map/psum | solution.py:34
  295.8 14.3 %multiply_reduce_fusion.4 = f32[256]{0:T(256)S(1)} fusion(f32[32768]{0:T(1024)S(1)} %multiply_divide_fusion.2, f32[256,32768]{1,0:T(8,128)} %get-tuple-element.18, f32[256]{0:T(256)S(1)} %get-tuple-element.12), kind=kLoop, calls=%fused_computation.7 | loop fusion | flops 25165568 | bytes 33687552 | tf_op jit(solution)/shard_map/reduce_sum | solution.py:37
  310.1 2.5 psum.65
  312.6 15.2 %multiply_reduce_fusion.3 = f32[32768]{0:T(1024)} fusion(f32[256]{0:T(256)S(1)} %multiply_divide_fusion.4, f32[256,32768]{1,0:T(8,128)} %get-tuple-element.18, f32[256]{0:T(256)S(1)} %get-tuple-element.12), kind=kLoop, calls=%fused_computation.6 | loop fusion | flops 25133056 | bytes 33687552 | tf_op jit(solution)/shard_map/reduce_sum | solution.py:33
  328.1 103.1 %all-reduce.8.cloned.1.call-done = f32[32768]{0:T(1024)} async-done(((f32[32768]{0:T(1024)}), f32[32768]{0:T(1024)}) %all-reduce.8.cloned.1.call-update) | async-done | bytes 131088 | tf_op jit(solution)/shard_map/psum | solution.py:34
  432.1 14.3 %multiply_reduce_fusion.2 = f32[256]{0:T(256)S(1)} fusion(f32[32768]{0:T(1024)S(1)} %multiply_divide_fusion.1, f32[256,32768]{1,0:T(8,128)} %get-tuple-element.18, f32[256]{0:T(256)S(1)} %get-tuple-element.12), kind=kLoop, calls=%fused_computation.5 | loop fusion | flops 25165568 | bytes 33687552 | tf_op jit(solution)/shard_map/reduce_sum | solution.py:37
  446.4 2.5 psum.67
  448.9 15.2 %multiply_reduce_fusion.1 = f32[32768]{0:T(1024)} fusion(f32[256]{0:T(256)S(1)} %multiply_divide_fusion.3, f32[256,32768]{1,0:T(8,128)} %get-tuple-element.18, f32[256]{0:T(256)S(1)} %get-tuple-element.12), kind=kLoop, calls=%fused_computation.4 | loop fusion | flops 25133056 | bytes 33687552 | tf_op jit(solution)/shard_map/reduce_sum | solution.py:33
  464.2 13.7 %exponential_reduce_fusion = f32[256]{0:T(256)S(1)} fusion(f32[256,32768]{1,0:T(8,128)} %get-tuple-element.16, f32[256]{0:T(256)S(1)} %get-tuple-element.11), kind=kLoop, calls=%fused_computation.10 | loop fusion | flops 16776960 | bytes 33556480 | tf_op jit(solution)/shard_map/reduce_sum | solution.py:46
  477.9 89.6 %all-reduce.10.cloned.1.call-done = f32[32768]{0:T(1024)} async-done(((f32[32768]{0:T(1024)}), f32[32768]{0:T(1024)}) %all-reduce.10.cloned.1.call-update) | async-done | bytes 131088 | tf_op jit(solution)/shard_map/psum | solution.py:34
  568.4 14.1 %multiply_reduce_fusion.6 = f32[256]{0:T(256)S(1)} fusion(f32[32768]{0:T(1024)S(1)} %multiply_divide_fusion, f32[256,32768]{1,0:T(8,128)} %get-tuple-element.18, f32[256]{0:T(256)S(1)} %get-tuple-element.12), kind=kLoop, calls=%fused_computation.11 | loop fusion | flops 25165568 | bytes 33687552 | tf_op jit(solution)/shard_map/reduce_sum | solution.py:37
  585.0 29.0 %multiply_convert_fusion = (bf16[256,32768]{1,0:T(8,128)(2,1)}, f32[256]{0:T(256)S(1)}) fusion(f32[256,32768]{1,0:T(8,128)} %get-tuple-element.16, f32[256]{0:T(256)S(1)} %get-tuple-element.9, f32[256]{0:T(256)S(1)} %get-tuple-element.11, f32[256]{0:T(256)S(1)} %divide_multiply_fusion, f32[32768]{0:T(1024)S(1)} %multiply_divide_fusion, ...), kind=kLoop, calls=%fused_computation.2 | loop fusion | flops 92274432 | bytes 84023296 | tf_op jit(solution)/shard_map/convert_element_type | solution.py:50
  614.0 13.6 %fusion = bf16[128,32768]{0,1:T(8,128)(2,1)} fusion(bf16[256,32768]{1,0:T(8,128)(2,1)} %get-tuple-element.13, bf16[256,128]{1,0:T(8,128)(2,1)S(1)} %copy-done), kind=kOutput, calls=%fused_computation.1 | convolution fusion | flops 2151677952 | bytes 25231360 | tf_op jit(solution)/shard_map/dot_general | solution.py:10
  627.6 12.2 %copy.8 = f32[128,32768]{1,0:T(8,128)} copy(bf16[128,32768]{0,1:T(8,128)(2,1)} %fusion) | data formatting | bytes 25165824
  639.9 2.5 psum.71
  642.9 342.5 %reduce-scatter.4.cloned.1.call-done = f32[8,32768]{1,0:T(8,128)} async-done(((f32[128,32768]{1,0:T(8,128)}), f32[8,32768]{1,0:T(8,128)}) %reduce-scatter.4.cloned.1.call-update) | async-done | bytes 1048592
  985.5 9.2 copy.9
  994.6 8.9 multiply_convert_fusion.1
  1003.6 6.8 copy.7
  (26 shorter events, 11.9 us)
Async XLA Ops:
  7.2 138.3 %copy-start = (bf16[256,128]{1,0:T(8,128)(2,1)S(1)}, bf16[256,128]{1,0:T(8,128)(2,1)}, u32[]{:S(2)}) copy-start(bf16[256,128]{1,0:T(8,128)(2,1)} %param.4) | copy-start | bytes 196612
  7.2 119.2 %all-gather.2.cloned.1.call-start = ((), (), s32[]{:S(2)}) async-start(), calls=%async_computation.1 | async-start | bytes 8912896 | tf_op jit(solution)/shard_map/all_gather | solution.py:21
  7.9 287.0 %all-reduce.6.cloned.1.call-start = ((), (), s32[]{:S(2)}) async-start(), calls=%async_computation.2 | async-start | bytes 262144 | tf_op jit(solution)/shard_map/psum | solution.py:34
  126.3 19.2 %copy-start.1 = (bf16[128,32768]{1,0:T(8,128)(2,1)S(1)}, bf16[128,32768]{1,0:T(8,128)(2,1)}, u32[]{:S(2)}) copy-start(bf16[128,32768]{1,0:T(8,128)(2,1)} %all-gather.2.cloned.1.call-done) | copy-start | bytes 25165828
  192.4 238.8 %all-reduce.8.cloned.1.call-start = ((), (), s32[]{:S(2)}) async-start(), calls=%async_computation.3 | async-start | bytes 262144 | tf_op jit(solution)/shard_map/psum | solution.py:34
  327.8 239.7 %all-reduce.10.cloned.1.call-start = ((), (), s32[]{:S(2)}) async-start(), calls=%async_computation.4 | async-start | bytes 262144 | tf_op jit(solution)/shard_map/psum | solution.py:34
  464.1 521.3 %reduce-scatter.4.cloned.1.call-start = ((), (), s32[]{:S(2)}) async-start(), calls=%async_computation.5 | async-start | bytes 17825792
Sparse Core Ops, SparseCore 0:
  10.8 115.5 all-gather.1
  192.5 102.3 all-reduce.5
  327.9 103.1 all-reduce.7
  464.2 103.2 all-reduce.9
  640.0 345.4 reduce-scatter.3
where the time goes:
time: 1020 us
  waiting for transfers between devices  757 us (74%)
  other arithmetic  157 us (15%)
  matrix products  45.8 us (4%)
  local copies, waits for them, and re-layouts  28.2 us (3%)
  blocking collectives  14.8 us (1%)
  between operations  13.8 us (1%)
    unnamed x6, waiting for transfers between devices  343 us
    psum x3, waiting for transfers between devices, column_scale(): return 1.0 / (protos_all * lax.psum(partial_value, 'dp'))  295 us
    all_gather x1, waiting for transfers between devices, shards(): shard_rows = lax.all_gather(prototypes, 'dp', axis=0, tiled=True)  118 us
    reduce_sum x3, other arithmetic, column_scale(): partial_value = jnp.sum(teach_exp * scale_in[:, None], axis=0)  45.7 us
    reduce_sum x3, other arithmetic, row_total(): return lax.psum(jnp.sum(weighted_in, axis=1), 'proto')  42.7 us
    convert_element_type x1, other arithmetic, shards(): logit_grad = (protos_all * (softmax_rows - targets)).astype(jnp.bfloat16)  29 us
    unnamed x7, local copies, waits for them, and re-layouts  28.2 us
  transfers between devices with their start and end apart: 5, of which 5 were waited for; matrix products, arithmetic and copies ran while one was open for 1% of the time, Pallas kernels for 0%

commit v1 on v0

v1 whole, which is shorter than its diff:
```python
import functools

import jax
import jax.numpy as jnp
from jax import lax
from jax.experimental import pallas as pl
from jax.experimental.pallas import tpu as pltpu
from jax.sharding import PartitionSpec as P

ITERS = 3
F32 = jnp.float32
BF16 = jnp.bfloat16
NT = (((1,), (1,)), ((), ()))


def params(mib=40):
    return pltpu.CompilerParams(
        vmem_limit_bytes=mib * 1024 * 1024, dimension_semantics=("arbitrary",)
    )


def full(shape):
    return pl.BlockSpec(shape, lambda i: (0,) * len(shape))


def split_hi_lo(v):
    hi = v.astype(BF16)
    return hi, (v - hi.astype(F32)).astype(BF16)


def exp_kernel(kc, protos, crops, x_out, peak_out, total_out, protos_t, scores):
    width = protos_t.shape[0]
    rb = crops.shape[0]

    @pl.when(pl.program_id(0) == 0)
    def _():
        for k in range(0, width, 128):
            protos_t[k : k + 128, :] = protos[:, k : k + 128].astype(F32).T.astype(BF16)

    peak = jnp.full((8, rb), -jnp.inf, F32)
    for k in range(0, width, kc):
        s = lax.dot_general(
            protos_t[k : k + kc, :], crops[...], NT, preferred_element_type=F32
        )
        scores[k : k + kc, :] = s
        peak = jnp.maximum(peak, jnp.max(s.reshape(kc // 8, 8, rb), axis=0))
    peak = jnp.max(peak, axis=0, keepdims=True)
    total = jnp.zeros((8, rb), F32)
    for k in range(0, width, kc):
        e = jnp.exp(scores[k : k + kc, :] - peak)
        total = total + jnp.sum(e.reshape(kc // 8, 8, rb), axis=0)
        x_out[k : k + kc, :] = e.astype(BF16)
    peak_out[...] = peak
    total_out[...] = jnp.sum(total, axis=0, keepdims=True)


def exp_rows(protos, crops):
    depth, width = protos.shape
    n = crops.shape[0]
    rb = 512
    kc = min(256, width)
    return pl.pallas_call(
        functools.partial(exp_kernel, kc),
        grid=(n // rb,),
        in_specs=[full((depth, width)), pl.BlockSpec((rb, depth), lambda i: (i, 0))],
        out_specs=[
            pl.BlockSpec((width, rb), lambda i: (0, i)),
            pl.BlockSpec((1, rb), lambda i: (0, i)),
            pl.BlockSpec((1, rb), lambda i: (0, i)),
        ],
        out_shape=[
            jax.ShapeDtypeStruct((width, n), BF16),
            jax.ShapeDtypeStruct((1, n), F32),
            jax.ShapeDtypeStruct((1, n), F32),
        ],
        scratch_shapes=[pltpu.VMEM((width, depth), BF16), pltpu.VMEM((width, rb), F32)],
        compiler_params=params(),
        cost_estimate=pl.CostEstimate(
            flops=2 * n * width * depth, bytes_accessed=2 * n * width, transcendentals=n * width
        ),
        name="exp_rows",
    )(protos, crops)


def sweep_kernel(protos_all, x, weight, factor, part_out, col_out, weights2, acc):
    step = pl.program_id(0)
    kb, n = x.shape

    @pl.when(step == 0)
    def _():
        hi, lo = split_hi_lo(weight[...])
        row = lax.broadcasted_iota(jnp.int32, (16, n), 0)
        hi = jnp.broadcast_to(hi.astype(F32), (16, n))
        lo = jnp.broadcast_to(lo.astype(F32), (16, n))
        weights2[...] = jnp.where(row == 0, hi, jnp.where(row == 1, lo, 0.0)).astype(BF16)
        acc[...] = jnp.zeros_like(acc)

    sums = lax.dot_general(x[...], weights2[...], NT, preferred_element_type=F32)
    col = 1.0 / (protos_all * jnp.sum(sums, axis=1, keepdims=True))
    col_out[...] = jnp.broadcast_to(col, (kb, 128)).T[:1, :]
    lanes = 512
    for r in range(0, n, lanes):
        v = x[:, r : r + lanes].astype(F32) * col
        acc[:, r : r + lanes] += jnp.sum(v.reshape(kb // 8, 8, lanes), axis=0)

    @pl.when(step == pl.num_programs(0) - 1)
    def _():
        part_out[...] = jnp.sum(acc[...], axis=0, keepdims=True) * factor[...]


def sweep(protos_all, x, weight, factor):
    width, n = x.shape
    kb = min(256, width)
    return pl.pallas_call(
        functools.partial(sweep_kernel, protos_all),
        grid=(width // kb,),
        in_specs=[pl.BlockSpec((kb, n), lambda i: (i, 0)), full((1, n)), full((1, n))],
        out_specs=[full((1, n)), pl.BlockSpec((1, kb), lambda i: (0, i))],
        out_shape=[
            jax.ShapeDtypeStruct((1, n), F32),
            jax.ShapeDtypeStruct((1, width), F32),
        ],
        scratch_shapes=[pltpu.VMEM((16, n), BF16), pltpu.VMEM((8, n), F32)],
        compiler_params=params(),
        cost_estimate=pl.CostEstimate(
            flops=4 * n * width, bytes_accessed=2 * n * width, transcendentals=0
        ),
        name="sweep",
    )(x, weight, factor)


def project_kernel(x, weight, student, out, weighted):
    n, depth = student.shape

    @pl.when(pl.program_id(0) == 0)
    def _():
        for r in range(0, n, 128):
            s = student[r : r + 128, :].astype(F32).T * weight[:, r : r + 128]
            hi, lo = split_hi_lo(s)
            weighted[:depth, r : r + 128] = hi
            weighted[depth:, r : r + 128] = lo

    g = lax.dot_general(x[...], weighted[...], NT, preferred_element_type=F32)
    out[...] = g[:, :depth] + g[:, depth:]


def project(x, weight, student):
    width, n = x.shape
    depth = student.shape[1]
    kb = min(256, width)
    return pl.pallas_call(
        project_kernel,
        grid=(width // kb,),
        in_specs=[pl.BlockSpec((kb, n), lambda i: (i, 0)), full((1, n)), full((n, depth))],
        out_specs=pl.BlockSpec((kb, depth), lambda i: (i, 0)),
        out_shape=jax.ShapeDtypeStruct((width, depth), F32),
        scratch_shapes=[pltpu.VMEM((2 * depth, n), BF16)],
        compiler_params=params(),
        cost_estimate=pl.CostEstimate(
            flops=2 * n * width * depth, bytes_accessed=2 * n * width, transcendentals=0
        ),
        name="project",
    )(x, weight, student)


def grad_kernel(scale, x, weight, student, first, col, out, weighted):
    n, depth = student.shape
    kb = x.shape[0]

    @pl.when(pl.program_id(0) == 0)
    def _():
        for r in range(0, n, 128):
            s = student[r : r + 128, :].astype(F32).T * weight[:, r : r + 128]
            hi, lo = split_hi_lo(s)
            weighted[:depth, r : r + 128] = hi
            weighted[depth:, r : r + 128] = lo

    g = lax.dot_general(x[...], weighted[...], NT, preferred_element_type=F32)
    g = g[:, :depth] + g[:, depth:]
    for k in range(0, kb, 128):
        a = first[k : k + 128, :].T
        b = g[k : k + 128, :].T
        out[:, k : k + 128] = (scale * (a - b * col[:, k : k + 128])).astype(BF16)


def proto_grad_columns(scale, x, weight, student, first, col):
    width, n = x.shape
    depth = student.shape[1]
    kb = min(256, width)
    return pl.pallas_call(
        functools.partial(grad_kernel, scale),
        grid=(width // kb,),
        in_specs=[
            pl.BlockSpec((kb, n), lambda i: (i, 0)),
            full((1, n)),
            full((n, depth)),
            pl.BlockSpec((kb, depth), lambda i: (i, 0)),
            pl.BlockSpec((1, kb), lambda i: (0, i)),
        ],
        out_specs=pl.BlockSpec((depth, kb), lambda i: (0, i)),
        out_shape=jax.ShapeDtypeStruct((depth, width), BF16),
        scratch_shapes=[pltpu.VMEM((2 * depth, n), BF16)],
        compiler_params=params(),
        cost_estimate=pl.CostEstimate(
            flops=2 * n * width * depth, bytes_accessed=2 * n * width, transcendentals=0
        ),
        name="proto_grad",
    )(x, weight, student, first, col)


def logit_kernel(protos_all, chunk, protos, crops, col, bias, grad_out, loss_out, bias_t, loss):
    step = pl.program_id(0)
    rows = grad_out.shape[0]
    width = protos.shape[1]

    @pl.when(step == 0)
    def _():
        bias_t[:rows, :] = jnp.broadcast_to(bias[0:1, :], (128, rows)).T
        bias_t[rows:, :] = jnp.broadcast_to(bias[1:2, :], (128, rows)).T
        loss[...] = jnp.zeros_like(loss)

    total = loss[...]
    for k in range(0, width, chunk):
        s = jnp.dot(crops[...], protos[:, k : k + chunk], preferred_element_type=F32)
        for j in range(0, chunk, 128):
            t = jnp.exp(s[:rows, j : j + 128] + bias_t[:rows, :]) * col[:, k + j : k + j + 128]
            log_probs = s[rows:, j : j + 128] + bias_t[rows:, :]
            g = protos_all * (jnp.exp(log_probs) - t)
            grad_out[:, k + j : k + j + 128] = g.astype(BF16)
            total = total + t * log_probs
    loss[...] = total

    @pl.when(step == pl.num_programs(0) - 1)
    def _():
        loss_out[...] = -jnp.sum(loss[...].T, axis=0, keepdims=True)


def logit_grads(protos_all, protos, crops, col, bias):
    depth, width = protos.shape
    rows = crops.shape[0] // 2
    cb = min(2048, width)
    return pl.pallas_call(
        functools.partial(logit_kernel, float(protos_all), min(256, cb)),
        grid=(width // cb,),
        in_specs=[
            pl.BlockSpec((depth, cb), lambda i: (0, i)),
            full((2 * rows, depth)),
            pl.BlockSpec((1, cb), lambda i: (0, i)),
            full((2, rows)),
        ],
        out_specs=[pl.BlockSpec((rows, cb), lambda i: (0, i)), full((1, rows))],
        out_shape=[
            jax.ShapeDtypeStruct((rows, width), BF16),
            jax.ShapeDtypeStruct((1, rows), F32),
        ],
        scratch_shapes=[pltpu.VMEM((2 * rows, 128), F32), pltpu.VMEM((rows, 128), F32)],
        compiler_params=params(),
        cost_estimate=pl.CostEstimate(
            flops=4 * rows * width * depth,
            bytes_accessed=2 * width * (rows + depth),
            transcendentals=2 * rows * width,
        ),
        name="logit_grads",
    )(protos, crops, col, bias)


def both(v):
    size = lax.axis_size("proto")
    if size == 2:
        return jnp.stack([v, lax.ppermute(v, "proto", [(0, 1), (1, 0)])])
    return lax.all_gather(v, "proto")


def from_all(v):
    size = lax.axis_size("dp")
    return lax.all_to_all(jnp.broadcast_to(v[None], (size,) + v.shape), "dp", 0, 0, tiled=True)


def merge(pairs):
    peak = jnp.max(pairs[:, 0], axis=0)
    total = jnp.sum(pairs[:, 1] * jnp.exp(pairs[:, 0] - peak), axis=0)
    return jnp.stack([peak, total])


def shards(teacher, student, prototypes):
    rows, depth = teacher.shape
    n = rows * lax.axis_size("dp")
    protos_all = prototypes.shape[1] * lax.axis_size("proto")
    gathered = lax.all_gather(prototypes, "dp", axis=0, tiled=True)
    own = lax.all_to_all(prototypes, "dp", 1, 0, tiled=True)
    teacher_all = from_all(teacher).reshape(n, depth)
    student_all = from_all(student).reshape(n, depth)

    x_t, peak_t, total_t = exp_rows(own, teacher_all)
    stats = from_all(merge(both(jnp.concatenate([peak_t, total_t]))))
    x_s, peak_s, total_s = exp_rows(own, student_all)
    stats = merge(stats)
    factor = jnp.exp(peak_t - stats[:1])
    weight = factor / stats[1:]
    glob_t = stats[:1]

    for it in range(ITERS):
        part, col = sweep(float(protos_all), x_t, weight, factor)
        if it == 0:
            st = merge(both(jnp.concatenate([peak_s, total_s])))
            got = from_all(jnp.concatenate([jnp.sum(both(part), axis=0), st]))
            total = jnp.sum(got[:, :1], axis=0)
            st = merge(got[:, 1:])
            glob_s, total_s = st[:1], st[1:]
            soft = project(x_s, jnp.exp(peak_s - glob_s) / total_s, student_all)
        elif it < ITERS - 1:
            total = jnp.sum(from_all(jnp.sum(both(part), axis=0)), axis=0)
        else:
            got = from_all(jnp.concatenate([jnp.sum(both(part), axis=0), col], axis=1))
            total = jnp.sum(got[:, :, :n], axis=0)
            col_all = got[:, 0, n:].reshape(1, -1)
        row_scale = 1.0 / (n * total)
        weight = row_scale * factor

    grad = proto_grad_columns(protos_all / 128.0, x_t, weight * n, student_all, soft, col)
    proto_grad = lax.all_to_all(grad, "dp", 0, 1, tiled=True)

    bias = jnp.concatenate([jnp.log(n * row_scale) - glob_t, -glob_s - jnp.log(total_s)])
    bias = lax.dynamic_slice_in_dim(bias, lax.axis_index("dp") * rows, rows, 1)
    logit_grad, loss = logit_grads(
        protos_all, gathered, jnp.concatenate([teacher, student]), col_all, bias
    )
    crop_loss = jnp.sum(both(loss[0]), axis=0)
    return crop_loss, logit_grad, proto_grad


def solution(mesh):
    placed = (P("dp", None), P("dp", None), P("dp", "proto"))
    return jax.shard_map(
        shards,
        mesh=mesh,
        in_specs=placed,
        out_specs=(P("dp"), P("dp", "proto"), P("dp", "proto")),
        check_vma=False,
    )
```

time: 1020 us -> 328 us (0.32)
  waiting for transfers between devices: 757 us -> 42.8 us
  other arithmetic: 157 us -> 3.58 us
  Pallas kernels: 0 us -> 111 us
  blocking collectives: 14.8 us -> 121 us
  matrix products: 45.8 us -> 0 us
  starting transfers between devices: 0.38 us -> 24.8 us
  local copies, waits for them, and re-layouts: 28.2 us -> 8.78 us
    unnamed x6 -> x1, waiting for transfers between devices: 343 us -> 0.68 us
    psum x3 -> x0, waiting for transfers between devices: 295 us -> none  [column_scale(): return 1.0 / (protos_all * lax.psum(partial_value, 'dp'))]
    all_to_all x0 -> x4, blocking collectives: none -> 121 us  [from_all(): lax.all_to_all(jnp.broadcast_to(v[None], (size,) + v.shape), 'dp', 0, 0,...]
    all_gather x1, waiting for transfers between devices: 118 us -> 0.01 us  [shards(): gathered = lax.all_gather(prototypes, 'dp', axis=0, tiled=True)]
    reduce_sum x8 -> x10, other arithmetic: 116 us -> 1.75 us  [the longest x4 0.83 us: merge(): total = jnp.sum(pairs[:, 1] * jnp.exp(pairs[:, 0] - peak), axis=0)]
    pallas_call x0 -> x8, Pallas kernels: none -> 111 us  [the longest x3 39.3 us: sweep(): pl.pallas_call(functools.partial(sweep_kernel, protos_all), grid=(width /...]
    dot_general x3 -> x0, matrix products: 45.8 us -> none  [the longest x1 19.2 us: shards(): jnp.dot(teacher, shard_rows, preferred_element_type=jnp.float32)]
    convert_element_type x2 -> x0, other arithmetic: 37.9 us -> none  [the longest x1 29 us: shards(): logit_grad = (protos_all * (softmax_rows - targets)).astype(jnp.bfloat16)]
  transfers between devices with their start and end apart: 5 -> 11, of which waited for: 5 -> 8; matrix products, arithmetic and copies ran while one was open for 1% -> 2% of each run, Pallas kernels for 0% -> 34%
where the time goes in v1:
time: 328 us; the launch traced here: 327 us
  blocking collectives  121 us (37%)
  Pallas kernels  111 us (34%)
  waiting for transfers between devices  42.8 us (13%)
  starting transfers between devices  24.8 us (8%)
  between operations  14.3 us (4%)
  local copies, waits for them, and re-layouts  8.78 us (3%)
  other arithmetic  3.58 us (1%)
    all_to_all x4, blocking collectives, from_all(): lax.all_to_all(jnp.broadcast_to(v[None], (size,) + v.shape), 'dp', 0, 0,...  121 us
    pallas_call x3, Pallas kernels, sweep(): pl.pallas_call(functools.partial(sweep_kernel, protos_all), grid=(width /...  39.3 us
    pallas_call x2, Pallas kernels, exp_rows(): pl.pallas_call(functools.partial(exp_kernel, kc), grid=(n // rb,), in_spe...  28.9 us
    all_to_all x2, waiting for transfers between devices, from_all(): lax.all_to_all(jnp.broadcast_to(v[None], (size,) + v.shape), 'dp', 0, 0,...  22.3 us
    pallas_call x1, Pallas kernels, logit_grads(): pl.pallas_call(functools.partial(logit_kernel, float(protos_all), min(256...  19.6 us
    all_to_all x1, waiting for transfers between devices, shards(): own = lax.all_to_all(prototypes, 'dp', 1, 0, tiled=True)  14.4 us
    pallas_call x1, Pallas kernels, proto_grad_columns(): pl.pallas_call(functools.partial(grad_kernel, scale), grid=(width // kb,)...  12.2 us
    pallas_call x1, Pallas kernels, project(): pl.pallas_call(project_kernel, grid=(width // kb,), in_specs=[pl.BlockSpe...  11.2 us
  transfers between devices with their start and end apart: 11, of which 8 were waited for; matrix products, arithmetic and copies ran while one was open for 2% of the time, Pallas kernels for 34%

profile of v1, /device:TPU:0, one launch (start us, length us, event | category | flops | bytes accessed | tf_op | source)
XLA Modules:
  0.0 326.8 jit_solution(17291894115505661664)
XLA Ops:
  7.2 8.3 %all-to-all-start = ((bf16[8,16,2048]{2,0,1:T(8,128)(2,1)}), bf16[8,16,2048]{2,0,1:T(8,128)(2,1)S(1)}, u32[]{:S(2)}, u32[]{:S(2)}) async-start(bf16[8,16,2048]{2,0,1:T(8,128)(2,1)} %bitcast.92), calls=%async_computation | async-start | bytes 1048576 | tf_op jit(solution)/shard_map/all_to_all | solution.py:290
  16.2 14.4 %all-to-all-done = bf16[8,16,2048]{2,0,1:T(8,128)(2,1)S(1)} async-done(((bf16[8,16,2048]{2,0,1:T(8,128)(2,1)}), bf16[8,16,2048]{2,0,1:T(8,128)(2,1)S(1)}, u32[]{:S(2)}, u32[]{:S(2)}) %all-to-all-start) | async-done | bytes 524320 | tf_op jit(solution)/shard_map/all_to_all | solution.py:290
  31.7 44.1 %all_to_all.68 = bf16[16,256,128]{2,1,0:T(8,128)(2,1)S(1)} all-to-all(bf16[16,256,128]{2,1,0:T(8,128)(2,1)S(1)} %broadcast_in_dim.16), channel_id=1, replica_groups=mesh['dp'=16,'proto'=2] {'dp'}, dimensions={0} | all-to-all | bytes 2097152 | tf_op jit(solution)/shard_map/all_to_all | solution.py:276
  75.8 2.0 broadcast_in_dim.14
  77.8 7.6 %all-to-all-start.1 = ((bf16[16,256,128]{2,1,0:T(8,128)(2,1)}), bf16[16,256,128]{2,1,0:T(8,128)(2,1)S(1)}, u32[]{:S(2)}, u32[]{:S(2)}) async-start(bf16[16,256,128]{2,1,0:T(8,128)(2,1)} %broadcast_in_dim.14), calls=%async_computation.1 | async-start | bytes 2097152 | tf_op jit(solution)/shard_map/all_to_all | solution.py:276
  85.4 14.5 %exp_rows.3 = (bf16[2048,4096]{1,0:T(8,128)(2,1)}, f32[1,4096]{1,0:T(1,128)S(1)}, f32[1,4096]{1,0:T(1,128)S(1)}) custom-call(bf16[128,2048]{1,0:T(8,128)(2,1)S(1)} %bitcast.87, bf16[4096,128]{1,0:T(8,128)(2,1)S(1)} %bitcast.83), custom_call_target="tpu_custom_call" | custom-call | flops 2147483648 | bytes 16777216 | tf_op jit(solution)/shard_map/exp_rows/pallas_call | solution.py:62
  100.0 20.5 %all-to-all-done.1 = bf16[16,256,128]{2,1,0:T(8,128)(2,1)S(1)} async-done(((bf16[16,256,128]{2,1,0:T(8,128)(2,1)}), bf16[16,256,128]{2,1,0:T(8,128)(2,1)S(1)}, u32[]{:S(2)}, u32[]{:S(2)}) %all-to-all-start.1) | async-done | bytes 1048608 | tf_op jit(solution)/shard_map/all_to_all | solution.py:276
  120.5 14.4 %exp_rows.2 = (bf16[2048,4096]{1,0:T(8,128)(2,1)}, f32[1,4096]{1,0:T(1,128)S(1)}, f32[1,4096]{1,0:T(1,128)S(1)}) custom-call(bf16[128,2048]{1,0:T(8,128)(2,1)S(1)} %bitcast.88, bf16[4096,128]{1,0:T(8,128)(2,1)S(1)} %bitcast.86), custom_call_target="tpu_custom_call" | custom-call | flops 2147483648 | bytes 16777216 | tf_op jit(solution)/shard_map/exp_rows/pallas_call | solution.py:62
  135.0 1.2 collective-permute-done
  136.7 32.0 %all_to_all.69 = f32[16,2,4096]{2,1,0:T(2,128)S(1)} all-to-all(f32[16,2,4096]{2,1,0:T(2,128)S(1)} %broadcast_in_dim.15), channel_id=1, replica_groups=mesh['dp'=16,'proto'=2] {'dp'}, dimensions={0} | all-to-all | bytes 1048576 | tf_op jit(solution)/shard_map/all_to_all | solution.py:276
  169.6 13.3 %sweep.3 = (f32[1,4096]{1,0:T(1,128)S(1)}, f32[1,2048]{1,0:T(1,128)}) custom-call(bf16[2048,4096]{1,0:T(8,128)(2,1)} %get-tuple-element.15.x, f32[1,4096]{1,0:T(1,128)S(1)} %get-tuple-element.29.weight, f32[1,4096]{1,0:T(1,128)S(1)} %get-tuple-element.30.factor), custom_call_target="tpu_custom_call" | custom-call | flops 33554432 | bytes 16777216 | tf_op jit(solution)/shard_map/sweep/pallas_call | solution.py:114
  184.4 31.1 %all_to_all.70 = f32[16,3,4096]{2,1,0:T(4,128)S(1)} all-to-all(f32[16,3,4096]{2,1,0:T(4,128)S(1)} %broadcast_in_dim.17), channel_id=1, replica_groups=mesh['dp'=16,'proto'=2] {'dp'}, dimensions={0} | all-to-all | bytes 1572864 | tf_op jit(solution)/shard_map/all_to_all | solution.py:276
  216.2 13.3 %sweep.4 = (f32[1,4096]{1,0:T(1,128)S(1)}, f32[1,2048]{1,0:T(1,128)}) custom-call(bf16[2048,4096]{1,0:T(8,128)(2,1)} %get-tuple-element.15.x, f32[1,4096]{1,0:T(1,128)S(1)} %mul.82.weight, f32[1,4096]{1,0:T(1,128)S(1)} %get-tuple-element.30.factor), custom_call_target="tpu_custom_call" | custom-call | flops 33554432 | bytes 16777216 | tf_op jit(solution)/shard_map/sweep/pallas_call | solution.py:114
  229.5 1.2 collective-permute-done.3
  230.9 13.9 %all_to_all.71 = f32[16,1,4096]{2,1,0:T(1,128)S(1)} all-to-all(f32[16,1,4096]{2,1,0:T(1,128)S(1)} %broadcast_in_dim.18), channel_id=1, replica_groups=mesh['dp'=16,'proto'=2] {'dp'}, dimensions={0} | all-to-all | bytes 524288 | tf_op jit(solution)/shard_map/all_to_all | solution.py:276
  245.1 12.7 %sweep.5 = (f32[1,4096]{1,0:T(1,128)S(1)}, f32[1,2048]{1,0:T(1,128)S(1)}) custom-call(bf16[2048,4096]{1,0:T(8,128)(2,1)} %get-tuple-element.15.x, f32[1,4096]{1,0:T(1,128)S(1)} %mul.84.weight, f32[1,4096]{1,0:T(1,128)S(1)} %get-tuple-element.30.factor), custom_call_target="tpu_custom_call" | custom-call | flops 33554432 | bytes 16777216 | tf_op jit(solution)/shard_map/sweep/pallas_call | solution.py:114
  260.1 3.6 %all-to-all-start.6 = ((f32[16,1,6144]{2,1,0:T(1,128)}), f32[16,1,6144]{2,1,0:T(1,128)S(1)}, u32[]{:S(2)}, u32[]{:S(2)}) async-start(f32[16,1,6144]{2,1,0:T(1,128)} %broadcast_in_dim.20), calls=%async_computation.6 | async-start | bytes 786432 | tf_op jit(solution)/shard_map/all_to_all | solution.py:276
  263.7 11.2 %project.1.first = f32[2048,128]{1,0:T(8,128)S(1)} custom-call(bf16[2048,4096]{1,0:T(8,128)(2,1)} %get-tuple-element.26.x, f32[1,4096]{1,0:T(1,128)S(1)} %get-tuple-element.44.weight, bf16[4096,128]{1,0:T(8,128)(2,1)S(1)} %bitcast.84), custom_call_target="tpu_custom_call" | custom-call | flops 2147483648 | bytes 16777216 | tf_op jit(solution)/shard_map/project/pallas_call | solution.py:151
  274.9 1.8 all-to-all-done.6
  277.0 12.2 %proto_grad.1 = bf16[128,2048]{1,0:T(8,128)(2,1)} custom-call(bf16[2048,4096]{1,0:T(8,128)(2,1)} %get-tuple-element.15.x, f32[1,4096]{1,0:T(1,128)S(1)} %get-tuple-element.50.weight, bf16[4096,128]{1,0:T(8,128)(2,1)S(1)} %bitcast.85, f32[2048,128]{1,0:T(8,128)S(1)} %project.1.first, f32[1,2048]{1,0:T(1,128)S(1)} %get-tuple-element.23.col), custom_call_target="tpu_custom_call" | custom-call | flops 2147483648 | bytes 16777216 | tf_op jit(solution)/shard_map/proto_grad/pallas_call | solution.py:190
  289.2 5.1 %all-to-all-start.7 = ((bf16[16,8,2048]{2,1,0:T(8,128)(2,1)}), bf16[16,8,2048]{2,1,0:T(8,128)(2,1)S(1)}, u32[]{:S(2)}, u32[]{:S(2)}) async-start(bf16[16,8,2048]{2,1,0:T(8,128)(2,1)} %bitcast.29), calls=%async_computation.7 | async-start | bytes 1048576 | tf_op jit(solution)/shard_map/all_to_all | solution.py:321
  294.4 3.4 %copy-done = bf16[128,32768]{1,0:T(8,128)(2,1)S(1)} copy-done((bf16[128,32768]{1,0:T(8,128)(2,1)S(1)}, bf16[128,32768]{1,0:T(8,128)(2,1)}, u32[]{:S(2)}) %copy-start) | copy-done | bytes 8388632
  297.8 19.6 %logit_grads.1 = (bf16[256,32768]{1,0:T(8,128)(2,1)}, f32[1,256]{1,0:T(1,128)S(1)}) custom-call(bf16[128,32768]{1,0:T(8,128)(2,1)S(1)} %copy-done, bf16[512,128]{1,0:T(8,128)(2,1)S(1)} %pad_maximum_fusion.crops, f32[1,32768]{1,0:T(1,128)S(1)} %bitcast.89, f32[2,256]{1,0:T(2,128)S(1)} %fusion.18.bias), custom_call_target="tpu_custom_call" | custom-call | flops 4294967296 | bytes 25165824 | tf_op jit(solution)/shard_map/logit_grads/pallas_call | solution.py:242
  317.4 1.1 collective-permute-done.5
  (53 shorter events, 9.8 us)
Async XLA Ops:
  7.2 23.5 %all-to-all-start = ((bf16[8,16,2048]{2,0,1:T(8,128)(2,1)}), bf16[8,16,2048]{2,0,1:T(8,128)(2,1)S(1)}, u32[]{:S(2)}, u32[]{:S(2)}) async-start(bf16[8,16,2048]{2,0,1:T(8,128)(2,1)} %bitcast.92), calls=%async_computation | async-start | bytes 1048576 | tf_op jit(solution)/shard_map/all_to_all | solution.py:290
  15.5 278.9 %all-gather.2.cloned.1.call-start = ((), (), s32[]{:S(2)}) async-start(), calls=%async_computation.8 | async-start | bytes 8912896 | tf_op jit(solution)/shard_map/all_gather | solution.py:289
  77.8 42.7 %all-to-all-start.1 = ((bf16[16,256,128]{2,1,0:T(8,128)(2,1)}), bf16[16,256,128]{2,1,0:T(8,128)(2,1)S(1)}, u32[]{:S(2)}, u32[]{:S(2)}) async-start(bf16[16,256,128]{2,1,0:T(8,128)(2,1)} %broadcast_in_dim.14), calls=%async_computation.1 | async-start | bytes 2097152 | tf_op jit(solution)/shard_map/all_to_all | solution.py:276
  100.0 35.1 %collective-permute-start.2 = (f32[2,4096]{1,0:T(2,128)S(1)}, f32[2,4096]{1,0:T(2,128)S(1)}, u32[]{:S(2)}, u32[]{:S(2)}) collective-permute-start(f32[2,4096]{1,0:T(2,128)S(1)} %get-tuple-element.49), channel_id=1, source_target_pairs={{0,1},{1,0},{2,3},{3,2},{4,5},{5,4},{6,7},{7,6},{8,9},{9,8},{10,11... | collective-permute-start | bytes 98312 | tf_op jit(solution)/shard_map/ppermute | solution.py:270
  134.9 1.3 collective-permute-start
  182.9 1.2 collective-permute-start.1
  229.5 1.2 collective-permute-start.3
  257.8 1.2 collective-permute-start.4
  260.1 16.7 %all-to-all-start.6 = ((f32[16,1,6144]{2,1,0:T(1,128)}), f32[16,1,6144]{2,1,0:T(1,128)S(1)}, u32[]{:S(2)}, u32[]{:S(2)}) async-start(f32[16,1,6144]{2,1,0:T(1,128)} %broadcast_in_dim.20), calls=%async_computation.6 | async-start | bytes 786432 | tf_op jit(solution)/shard_map/all_to_all | solution.py:276
  263.7 30.6 %copy-start.1 = (bf16[256,128]{1,0:T(8,128)(2,1)S(1)}, bf16[256,128]{1,0:T(8,128)(2,1)}, u32[]{:S(2)}) copy-start(bf16[256,128]{1,0:T(8,128)(2,1)} %param.4) | copy-start | bytes 196612
  263.7 30.6 %copy-start.2 = (bf16[256,128]{1,0:T(8,128)(2,1)S(1)}, bf16[256,128]{1,0:T(8,128)(2,1)}, u32[]{:S(2)}) copy-start(bf16[256,128]{1,0:T(8,128)(2,1)} %param.3) | copy-start | bytes 196612
  289.2 28.2 %all-to-all-start.7 = ((bf16[16,8,2048]{2,1,0:T(8,128)(2,1)}), bf16[16,8,2048]{2,1,0:T(8,128)(2,1)S(1)}, u32[]{:S(2)}, u32[]{:S(2)}) async-start(bf16[16,8,2048]{2,1,0:T(8,128)(2,1)} %bitcast.29), calls=%async_computation.7 | async-start | bytes 1048576 | tf_op jit(solution)/shard_map/all_to_all | solution.py:321
  294.4 3.4 %copy-start = (bf16[128,32768]{1,0:T(8,128)(2,1)S(1)}, bf16[128,32768]{1,0:T(8,128)(2,1)}, u32[]{:S(2)}) copy-start(bf16[128,32768]{1,0:T(8,128)(2,1)} %all-gather.2.cloned.1.call-done.protos) | copy-start | bytes 25165828
  317.4 1.1 collective-permute-start.5
Sparse Core Ops, SparseCore 0:
  19.1 140.0 all-gather.1
